TPU v7x, 32 devices: a whole 2x2x4 slice. The times are simulated.
32 devices in a mesh: dp: 4 (over y, x), tensor: 8 (over z, core).
Axes of the slice: x: 2, y: 2, z: 4, core: 2. Of those that a mesh axis runs over, the one named last changes fastest.
Arguments:
- tokens: bfloat16 [2048, 8192], P(('dp', 'tensor')), may hold values from -6 to 6
- w_query: bfloat16 [8192, 8192], P(None, 'tensor'), may hold values from -0.0625 to 0.0625
- cotangent: bfloat16 [2048, 8192], P('dp', 'tensor'), may hold values from -6 to 6
- task_embed: bfloat16 [128, 1024], replicated, may hold values from -6 to 6
- w_hidden: bfloat16 [1024, 512], P(None, 'tensor'), may hold values from -0.1875 to 0.1875
- head_a: bfloat16 [512, 16, 8192], P(None, 'dp', 'tensor'), may hold values from -0.0234375 to 0.0234375
- head_b: bfloat16 [512, 16, 8192], P(None, 'dp', 'tensor'), may hold values from -0.0234375 to 0.0234375
- block_task: int32 [4], replicated, may hold values from 0 to 127
Outputs:
- output: bfloat16 [2048, 8192], P('dp', 'tensor')
- grad_tokens: bfloat16 [2048, 8192], P(('dp', 'tensor'))
- grad_head_a: bfloat16 [512, 16, 8192], P(None, 'dp', 'tensor')
- grad_head_b: bfloat16 [512, 16, 8192], P(None, 'dp', 'tensor')
All inputs are finite; a program needn't handle non-finite values.
Results may differ from a plain program's by a relative error of at most 0.0077.
Values may be sent and summed in bfloat16 or wider, within the bound.
A program may use at most 128 MiB of HBM per device.

v0:
```python
import jax
import jax.numpy as jnp
from jax import lax
from jax.sharding import PartitionSpec as P


def local(tokens, w_query, cotangent, task_embed, w_hidden, head_a, head_b, block_task):
    single_float = jnp.float32
    brain_half_float = jnp.bfloat16
    n_groups = lax.axis_size("dp")
    n_shards = lax.axis_size("tensor")
    shard = lax.axis_index("tensor")
    hid_count, rank_rows, width = head_a.shape
    blocks = block_task.shape[0]
    per_group = blocks // n_groups
    hid_part = jax.nn.silu(
        jnp.dot(task_embed, w_hidden, preferred_element_type=single_float)
    ).astype(brain_half_float)
    hidden = lax.all_gather(hid_part, "tensor", axis=1, tiled=True)
    flat_a = head_a.reshape(hid_count, rank_rows * width)
    flat_b = head_b.reshape(hid_count, rank_rows * width)
    hid_blocks = hidden[block_task]
    gen_a = (
        jnp.dot(hid_blocks, flat_a, preferred_element_type=single_float)
        .astype(brain_half_float)
        .reshape(n_groups, per_group, rank_rows, width)
    )
    gen_b = (
        jnp.dot(hid_blocks, flat_b, preferred_element_type=single_float)
        .astype(brain_half_float)
        .reshape(n_groups, per_group, rank_rows, width)
    )
    recv_a, recv_b = (
        lax.all_to_all(gen_a, "dp", split_axis=0, concat_axis=2, tiled=True),
        lax.all_to_all(gen_b, "dp", split_axis=0, concat_axis=2, tiled=True),
    )
    adapter_down_weight = recv_a.reshape(per_group, rank_rows * n_groups, width)
    adapter_up_weight = recv_b.reshape(per_group, rank_rows * n_groups, width)
    rank = adapter_down_weight.shape[1]
    whole = lax.all_gather(tokens, "tensor", axis=0, tiled=True)
    rows_all, model_width = whole.shape
    block = rows_all // per_group
    rows_dev = rows_all // n_shards
    block_inputs = whole.reshape(per_group, block, model_width)
    input_columns = lax.dynamic_slice_in_dim(block_inputs, shard * width, width, 2)
    frozen_output = jnp.dot(whole, w_query, preferred_element_type=single_float)
    down_portion = jnp.einsum(
        "grs,gps->grp", input_columns, adapter_down_weight, preferred_element_type=single_float
    )
    down_projection = lax.psum(down_portion, "tensor")
    down_low_rank = down_projection.astype(brain_half_float)
    low_rank_update = jnp.einsum(
        "elm,emn->eln", down_low_rank, adapter_up_weight, preferred_element_type=single_float
    ).reshape(rows_all, width)
    output = (frozen_output + low_rank_update).astype(brain_half_float)
    block_output_grads = cotangent.reshape(per_group, block, width)
    backward_portion = jnp.einsum(
        "grs,gps->grp", block_output_grads, adapter_up_weight, preferred_element_type=single_float
    )
    backward_input = lax.psum(backward_portion, "tensor")
    backward_low_rank = backward_input.astype(brain_half_float)
    grad_sum = lax.psum_scatter(
        lax.dot_general(
            cotangent, w_query, (((1,), (1,)), ((), ())), preferred_element_type=single_float
        ),
        "tensor",
        scatter_dimension=0,
        tiled=True,
    )
    full_a = lax.all_gather(adapter_down_weight, "tensor", axis=2, tiled=True)
    first = shard * rows_dev
    which = first // block
    a_here = lax.dynamic_index_in_dim(full_a, which, 0, keepdims=False)
    back_rows = lax.dynamic_slice_in_dim(
        backward_low_rank.reshape(rows_all, rank), first, rows_dev, 0
    )
    grad_sum = grad_sum + jnp.dot(back_rows, a_here, preferred_element_type=single_float)
    grad_tokens = grad_sum.astype(brain_half_float)
    scale_average = 1.0 / block
    down_gradient = (
        jnp.einsum(
            "evr,evx->erx", backward_low_rank, input_columns, preferred_element_type=single_float
        )
        * scale_average
    ).astype(brain_half_float)
    up_gradient = (
        jnp.einsum(
            "evr,evx->erx", down_low_rank, block_output_grads, preferred_element_type=single_float
        )
        * scale_average
    ).astype(brain_half_float)
    back_a, back_b = (
        lax.all_to_all(down_gradient[None], "dp", split_axis=2, concat_axis=0, tiled=True),
        lax.all_to_all(up_gradient[None], "dp", split_axis=2, concat_axis=0, tiled=True),
    )
    head_grad_a = lax.dot_general(
        hid_blocks,
        back_a.reshape(blocks, rank_rows * width),
        (((0,), (0,)), ((), ())),
        preferred_element_type=single_float,
    )
    head_grad_b = lax.dot_general(
        hid_blocks,
        back_b.reshape(blocks, rank_rows * width),
        (((0,), (0,)), ((), ())),
        preferred_element_type=single_float,
    )
    grad_head_a = head_grad_a.reshape(hid_count, rank_rows, width).astype(brain_half_float)
    grad_head_b = head_grad_b.reshape(hid_count, rank_rows, width).astype(brain_half_float)
    return (output, grad_tokens, grad_head_a, grad_head_b)


def solution(mesh):
    return jax.shard_map(
        local,
        mesh=mesh,
        in_specs=(
            P(("dp", "tensor"), None),
            P(None, "tensor"),
            P("dp", "tensor"),
            P(),
            P(None, "tensor"),
            P(None, "dp", "tensor"),
            P(None, "dp", "tensor"),
            P(),
        ),
        out_specs=(
            P("dp", "tensor"),
            P(("dp", "tensor"), None),
            P(None, "dp", "tensor"),
            P(None, "dp", "tensor"),
        ),
        check_vma=False,
    )
```

profile of v0, /device:TPU:0, one launch (start us, length us, event | category | flops | bytes accessed | tf_op | source)
XLA Modules:
  0.0 277.4 jit_solution(17457322561264145729)
XLA Ops:
  8.4 15.9 %fusion.21 = f32[512,8192]{1,0:T(8,128)} fusion(bf16[512,1024]{1,0:T(8,128)(2,1)S(1)} %copy-done, bf16[8192,1024]{1,0:T(8,128)(2,1)} %param.9), kind=kOutput, calls=%fused_computation.39 | convolution fusion | flops 8589934592 | bytes 34603008 | tf_op jit(solution)/shard_map/dot_general | solution.py:63
  24.3 0.9 copy-done.1
  25.5 15.7 %all_gather.10 = bf16[128,512]{0,1:T(8,128)(2,1)S(1)} all-gather(bf16[128,64]{0,1:T(8,128)(2,1)S(1)} %multiply_convert_fusion), channel_id=1, replica_groups=mesh['dp'=4,'tensor'=8] {'tensor'}, dimensions={1}, use_global_device_ids=true | all-gather | bytes 147456 | tf_op jit(solution)/shard_map/all_gather | solution.py:19
  41.4 6.5 %copy.29 = bf16[64,8,4,1024]{3,1,2,0:T(8,128)(2,1)} copy(bf16[64,8,4,1024]{3,2,1,0:T(4,128)(2,1)} %bitcast.70) | data formatting | bytes 8388608
  48.5 2.9 %convolution_convert_fusion.1 = bf16[4,4096]{1,0:T(4,128)(2,1)S(1)} fusion(bf16[4,512]{1,0:T(4,128)(2,1)S(1)} %gather_fusion, bf16[512,4096]{1,0:T(8,128)(2,1)} %bitcast.68), kind=kOutput, calls=%fused_computation.4 | convolution fusion | flops 16793600 | bytes 4231168 | tf_op jit(solution)/shard_map/dot_general | solution.py:24
  52.0 3.7 %all-to-all-start = ((bf16[4,1,4,1024]{3,2,1,0:T(4,128)(2,1)}), bf16[4,1,4,1024]{3,2,1,0:T(4,128)(2,1)S(1)}, u32[]{:S(2)}, u32[]{:S(2)}) async-start(bf16[4,1,4,1024]{3,2,1,0:T(4,128)(2,1)} %bitcast), calls=%async_computation | async-start | bytes 65536 | tf_op jit(solution)/shard_map/all_to_all | solution.py:34
  55.8 4.6 %copy.30 = bf16[64,8,4,1024]{3,1,2,0:T(8,128)(2,1)S(1)} copy(bf16[64,8,4,1024]{3,2,1,0:T(4,128)(2,1)} %bitcast.71) | data formatting | bytes 8388608
  61.6 4.2 %all-to-all-start.1 = ((bf16[4,1,4,1024]{3,2,1,0:T(4,128)(2,1)}), bf16[4,1,4,1024]{3,2,1,0:T(4,128)(2,1)S(1)}, u32[]{:S(2)}, u32[]{:S(2)}) async-start(bf16[4,1,4,1024]{3,2,1,0:T(4,128)(2,1)} %bitcast.3), calls=%async_computation.1 | async-start | bytes 65536 | tf_op jit(solution)/shard_map/all_to_all | solution.py:35
  65.9 4.7 %all-to-all-done.1 = bf16[4,1,4,1024]{3,2,1,0:T(4,128)(2,1)S(1)} async-done(((bf16[4,1,4,1024]{3,2,1,0:T(4,128)(2,1)}), bf16[4,1,4,1024]{3,2,1,0:T(4,128)(2,1)S(1)}, u32[]{:S(2)}, u32[]{:S(2)}) %all-to-all-start.1) | async-done | bytes 32800 | tf_op jit(solution)/shard_map/all_to_all | solution.py:35
  70.6 17.4 %all_gather.11 = bf16[1,16,8192]{2,1,0:T(8,128)(2,1)S(1)} all-gather(bf16[1,16,1024]{2,1,0:T(8,128)(2,1)S(1)} %reshape.100), channel_id=1, replica_groups=mesh['dp'=4,'tensor'=8] {'tensor'}, dimensions={2}, use_global_device_ids=true | all-gather | bytes 294912 | tf_op jit(solution)/shard_map/all_gather | solution.py:70
  88.4 9.0 %all-gather.2.cloned.1.call-done = bf16[512,8192]{1,0:T(8,128)(2,1)} async-done(((bf16[64,8192]{1,0:T(8,128)(2,1)}), bf16[512,8192]{1,0:T(8,128)(2,1)}) %all-gather.2.cloned.1.call-update) | async-done | bytes 8388624 | tf_op jit(solution)/shard_map/all_gather | solution.py:40
  97.4 1.6 convolution_bitcast_fusion.1
  99.0 28.0 %all-reduce = (bf16[1,512,16]{1,2,0:T(8,128)(2,1)S(1)}, bf16[1,512,16]{1,2,0:T(8,128)(2,1)S(1)}) all-reduce(f32[1,512,16]{1,2,0:T(8,128)S(1)} %convolution_bitcast_fusion.1, f32[1,512,16]{1,2,0:T(8,128)S(1)} %convolution_bitcast_fusion), channel_id=1, replica_groups=mesh['dp'=4,'tensor'=8] {'tensor'}, use_global_device_ids=true, to_apply=%region_0.1 | all-reduce | flops 16384 | bytes 98304 | tf_op jit(solution)/shard_map/psum | solution.py:50
  127.0 1.5 fusion.4
  130.5 4.1 %all-to-all-start.2 = ((bf16[4,2,2048]{2,1,0:T(2,128)(2,1)}), bf16[4,2,2048]{2,1,0:T(2,128)(2,1)S(1)}, u32[]{:S(2)}, u32[]{:S(2)}) async-start(bf16[4,2,2048]{2,1,0:T(2,128)(2,1)} %reshape.116), calls=%async_computation.3 | async-start | bytes 65536 | tf_op jit(solution)/shard_map/all_to_all | solution.py:93
  135.1 15.7 %add_convert_fusion = bf16[512,1024]{1,0:T(8,128)(2,1)} fusion(f32[512,1024]{1,0:T(8,128)S(1)} %fusion.10, bf16[512,8192]{1,0:T(8,128)(2,1)} %all-gather.2.cloned.1.call-done, bf16[8192,1024]{1,0:T(8,128)(2,1)} %param.9), kind=kOutput, calls=%fused_computation.7 | convolution fusion | flops 8590983168 | bytes 28311552 | tf_op jit(solution)/shard_map/dot_general | solution.py:46
  151.1 0.8 reduce.5
  152.5 4.2 %all-to-all-start.3 = ((bf16[4,2,2048]{2,1,0:T(2,128)(2,1)}), bf16[4,2,2048]{2,1,0:T(2,128)(2,1)S(1)}, u32[]{:S(2)}, u32[]{:S(2)}) async-start(bf16[4,2,2048]{2,1,0:T(2,128)(2,1)} %reshape.118), calls=%async_computation.4 | async-start | bytes 65536 | tf_op jit(solution)/shard_map/all_to_all | solution.py:94
  157.0 1.3 convolution_convert_fusion.3
  158.3 5.2 %copy.27 = bf16[512,4,1024]{2,1,0:T(4,128)(2,1)} copy(bf16[512,4,1024]{2,0,1:T(8,128)(2,1)S(1)} %convolution_convert_fusion.3) | data formatting | bytes 8388608
  163.8 1.3 convolution_convert_fusion.2
  165.1 5.2 %copy.28 = bf16[512,4,1024]{2,1,0:T(4,128)(2,1)} copy(bf16[512,4,1024]{2,0,1:T(8,128)(2,1)S(1)} %convolution_convert_fusion.2) | data formatting | bytes 8388608
  170.4 97.1 %reduce-scatter.2.cloned.1.call-done = f32[64,8192]{1,0:T(8,128)} async-done(((f32[512,8192]{1,0:T(8,128)}), f32[64,8192]{1,0:T(8,128)}) %reduce-scatter.2.cloned.1.call-update) | async-done | bytes 2097168 | tf_op jit(solution)/shard_map/reduce_scatter | solution.py:62
  267.5 3.1 %fusion = bf16[64,8192]{1,0:T(8,128)(2,1)} fusion(f32[64,8192]{1,0:T(8,128)} %reduce-scatter.2.cloned.1.call-done, bf16[1,16,8192]{2,1,0:T(8,128)(2,1)S(1)} %all_gather.11, bf16[1,512,16]{1,2,0:T(8,128)(2,1)S(1)} %get-tuple-element.17, s32[]{:T(128)S(6)} %select_n.16), kind=kOutput, calls=%fused_computation.2 | convolution fusion | flops 17825792 | bytes 3411972 | tf_op jit(solution)/shard_map/dot_general | solution.py:77
  (40 shorter events, 8.5 us)
Async XLA Ops:
  7.2 1.2 copy-start
  7.2 90.2 %all-gather.2.cloned.1.call-start = ((), (), s32[]{:S(2)}) async-start(), calls=%async_computation.5 | async-start | bytes 9437184 | tf_op jit(solution)/shard_map/all_gather | solution.py:40
  7.9 259.6 %reduce-scatter.2.cloned.1.call-start = ((), (), s32[]{:S(2)}) async-start(), calls=%async_computation.6 | async-start | bytes 18874368 | tf_op jit(solution)/shard_map/reduce_scatter | solution.py:62
  24.3 0.9 copy-start.1
  24.3 1.0 copy-start.2
  41.4 6.5 %copy-start.3 = (s32[4]{0:T(128)S(1)}, s32[4]{0:T(128)}, u32[]{:S(2)}) copy-start(s32[4]{0:T(128)} %param.15) | copy-start | bytes 52
  52.0 9.6 %all-to-all-start = ((bf16[4,1,4,1024]{3,2,1,0:T(4,128)(2,1)}), bf16[4,1,4,1024]{3,2,1,0:T(4,128)(2,1)S(1)}, u32[]{:S(2)}, u32[]{:S(2)}) async-start(bf16[4,1,4,1024]{3,2,1,0:T(4,128)(2,1)} %bitcast), calls=%async_computation | async-start | bytes 65536 | tf_op jit(solution)/shard_map/all_to_all | solution.py:34
  61.6 9.0 %all-to-all-start.1 = ((bf16[4,1,4,1024]{3,2,1,0:T(4,128)(2,1)}), bf16[4,1,4,1024]{3,2,1,0:T(4,128)(2,1)S(1)}, u32[]{:S(2)}, u32[]{:S(2)}) async-start(bf16[4,1,4,1024]{3,2,1,0:T(4,128)(2,1)} %bitcast.3), calls=%async_computation.1 | async-start | bytes 65536 | tf_op jit(solution)/shard_map/all_to_all | solution.py:35
  130.5 22.0 %all-to-all-start.2 = ((bf16[4,2,2048]{2,1,0:T(2,128)(2,1)}), bf16[4,2,2048]{2,1,0:T(2,128)(2,1)S(1)}, u32[]{:S(2)}, u32[]{:S(2)}) async-start(bf16[4,2,2048]{2,1,0:T(2,128)(2,1)} %reshape.116), calls=%async_computation.3 | async-start | bytes 65536 | tf_op jit(solution)/shard_map/all_to_all | solution.py:93
  152.5 11.0 %all-to-all-start.3 = ((bf16[4,2,2048]{2,1,0:T(2,128)(2,1)}), bf16[4,2,2048]{2,1,0:T(2,128)(2,1)S(1)}, u32[]{:S(2)}, u32[]{:S(2)}) async-start(bf16[4,2,2048]{2,1,0:T(2,128)(2,1)} %reshape.118), calls=%async_computation.4 | async-start | bytes 65536 | tf_op jit(solution)/shard_map/all_to_all | solution.py:94
Sparse Core Ops, SparseCore 0:
  9.6 87.7 all-gather.1
  99.7 167.7 reduce-scatter.1
where the time goes:
time: 278 us; the launch traced here: 277 us
  waiting for transfers between devices  112 us (40%)
  blocking collectives  61.1 us (22%)
  matrix products  45.2 us (16%)
  local copies, waits for them, and re-layouts  27.4 us (10%)
  starting transfers between devices  16.3 us (6%)
  between operations  14.1 us (5%)
    reduce_scatter x1, waiting for transfers between devices, local(): lax.psum_scatter(lax.dot_general(cotangent, w_query, (((1,), (1,)), ((),...  97.1 us
    psum x1, blocking collectives, local(): down_projection = lax.psum(down_portion, 'tensor')  28 us
    unnamed x17, local copies, waits for them, and re-layouts  24.8 us
    all_gather x1, blocking collectives, local(): full_a = lax.all_gather(adapter_down_weight, 'tensor', axis=2, tiled=True)  17.4 us
    dot_general x1, matrix products, local(): lax.dot_general(cotangent, w_query, (((1,), (1,)), ((), ())), preferred_e...  15.9 us
    all_gather x1, blocking collectives, local(): hidden = lax.all_gather(hid_part, 'tensor', axis=1, tiled=True)  15.7 us
    dot_general x1, matrix products, local(): frozen_output = jnp.dot(whole, w_query, preferred_element_type=single_float)  15.7 us
    all_gather x1, waiting for transfers between devices, local(): whole = lax.all_gather(tokens, 'tensor', axis=0, tiled=True)  9.01 us
  transfers between devices with their start and end apart: 6, of which 3 were waited for; matrix products, arithmetic and copies ran while one was open for 25% of the time, Pallas kernels for 0%

commit v1 on v0

v1 whole, which is shorter than its diff:
```python
import functools

import jax
import jax.numpy as jnp
from jax import lax
from jax.experimental import pallas as pl
from jax.experimental.pallas import tpu as pltpu
from jax.sharding import PartitionSpec as P

F32 = jnp.float32
BF16 = jnp.bfloat16
MESH = pl.DeviceIdType.MESH
GRAD_CHUNKS = 8
SKEW = 2


def exchange_kernel(axis, n, scatter, x_ref, out_ref, send_sem, recv_sem):
    me = lax.axis_index(axis)
    barrier = pltpu.get_barrier_semaphore()
    for k in range(1, n):
        pl.semaphore_signal(
            barrier, inc=1, device_id={axis: lax.rem(me + k, n)}, device_id_type=MESH
        )
    pl.semaphore_wait(barrier, n - 1)
    copies = []
    for k in range(1, n):
        target = lax.rem(me + k, n)
        copy = pltpu.make_async_remote_copy(
            src_ref=x_ref.at[target] if scatter else x_ref,
            dst_ref=out_ref.at[me],
            send_sem=send_sem.at[k],
            recv_sem=recv_sem.at[k],
            device_id={axis: target},
            device_id_type=MESH,
        )
        copy.start()
        copies.append(copy)
    out_ref[me] = x_ref[me] if scatter else x_ref[...]
    for copy in copies:
        copy.wait()


def exchange(x, axis, n, scatter, cid):
    rows, lanes = x.shape[-2:]
    x = x.astype(F32)
    x = jnp.pad(x, [(0, 0)] * (x.ndim - 2) + [(0, -rows % 8), (0, -lanes % 128)])
    shape = x.shape if scatter else (n,) + x.shape
    got = pl.pallas_call(
        functools.partial(exchange_kernel, axis, n, scatter),
        out_shape=jax.ShapeDtypeStruct(shape, x.dtype),
        in_specs=[pl.BlockSpec(memory_space=pltpu.VMEM)],
        out_specs=pl.BlockSpec(memory_space=pltpu.VMEM),
        scratch_shapes=[pltpu.SemaphoreType.DMA((n,)), pltpu.SemaphoreType.DMA((n,))],
        compiler_params=pltpu.CompilerParams(collective_id=cid, has_side_effects=True),
    )(x)
    return got[..., :rows, :lanes]


def gradient_kernel(n, chunks, g_ref, w_ref, out_ref, w_buf, mine, give, theirs, up_out, up_in, down_out, down_in,
                    w_sem, pair_send, pair_recv, up_send, up_recv, down_send, down_recv):
    shard = lax.axis_index("tensor")
    z, core = shard // 2, lax.rem(shard, 2)
    chips = n // 2
    steps = chips - 1
    rows = out_ref.shape[0]
    cw = w_buf.shape[1]
    pair = {"tensor": 2 * z + 1 - core}
    above = {"tensor": lax.rem(shard + 2, n)}
    below = {"tensor": lax.rem(shard + n - 2, n)}
    has_above, has_below = z < chips - 1, z > 0

    barrier = pltpu.get_barrier_semaphore()
    pl.semaphore_signal(barrier, inc=1, device_id=pair, device_id_type=MESH)

    @pl.when(has_above)
    def _():
        pl.semaphore_signal(barrier, inc=1, device_id=above, device_id_type=MESH)

    @pl.when(has_below)
    def _():
        pl.semaphore_signal(barrier, inc=1, device_id=below, device_id_type=MESH)

    def fetch(c):
        slot = lax.rem(c, 2)
        return pltpu.make_async_copy(
            w_ref.at[pl.ds(pl.multiple_of(c * cw, cw), cw)], w_buf.at[slot], w_sem.at[slot]
        )

    fetch(0).start()
    pl.semaphore_wait(
        barrier, 1 + jnp.where(has_above, 1, 0) + jnp.where(has_below, 1, 0)
    )

    def pair_copy(c):
        return pltpu.make_async_remote_copy(
            src_ref=give.at[c],
            dst_ref=theirs.at[c],
            send_sem=pair_send.at[c],
            recv_sem=pair_recv.at[c],
            device_id=pair,
            device_id_type=MESH,
        )

    def up_copy(c, s):
        return pltpu.make_async_remote_copy(
            src_ref=up_out.at[c, s],
            dst_ref=up_in.at[c, s],
            send_sem=up_send.at[c, s],
            recv_sem=up_recv.at[c, s],
            device_id=above,
            device_id_type=MESH,
        )

    def down_copy(c, s):
        return pltpu.make_async_remote_copy(
            src_ref=down_out.at[c, s],
            dst_ref=down_in.at[c, s],
            send_sem=down_send.at[c, s],
            recv_sem=down_recv.at[c, s],
            device_id=below,
            device_id_type=MESH,
        )

    def product(i, w):
        return lax.dot_general(
            g_ref[i], w, (((1,), (1,)), ((), ())), preferred_element_type=F32
        ).astype(BF16).reshape(chips, rows, cw)

    def multiply(c):
        @pl.when(c + 1 < chunks)
        def _():
            fetch(c + 1).start()

        fetch(c).wait()
        w = w_buf[lax.rem(c, 2)]
        give[c] = product(0, w)
        pair_copy(c).start()
        mine[c] = product(1, w)

    def both(c, d):
        return mine[c, d].astype(F32) + theirs[c, d].astype(F32)

    def forward(c, s):
        if s == 0:
            pair_copy(c).wait_recv()
        far = steps - s

        @pl.when(z <= s)
        def _():
            total = both(c, z + far)
            if s == 0:
                up_out[c, s] = total.astype(BF16)
            else:
                @pl.when(has_below)
                def _():
                    up_copy(c, s - 1).wait_recv()
                    up_out[c, s] = (total + up_in[c, s - 1].astype(F32)).astype(BF16)

                @pl.when(jnp.logical_not(has_below))
                def _():
                    up_out[c, s] = total.astype(BF16)
            up_copy(c, s).start()

        @pl.when(z >= far)
        def _():
            total = both(c, z - far)
            if s == 0:
                down_out[c, s] = total.astype(BF16)
            else:
                @pl.when(has_above)
                def _():
                    down_copy(c, s - 1).wait_recv()
                    down_out[c, s] = (total + down_in[c, s - 1].astype(F32)).astype(BF16)

                @pl.when(jnp.logical_not(has_above))
                def _():
                    down_out[c, s] = total.astype(BF16)
            down_copy(c, s).start()

    def finish(c):
        columns = pl.ds(pl.multiple_of(c * cw, cw), cw)
        if steps == 0:
            pair_copy(c).wait_recv()
        out_ref[:, columns] = both(c, z)
        if steps:
            @pl.when(has_below)
            def _():
                up_copy(c, steps - 1).wait_recv()
                out_ref[:, columns] += up_in[c, steps - 1].astype(F32)

            @pl.when(has_above)
            def _():
                down_copy(c, steps - 1).wait_recv()
                out_ref[:, columns] += down_in[c, steps - 1].astype(F32)

    def at(c, stage):
        @pl.when(jnp.logical_and(c >= 0, c < chunks))
        def _():
            stage(c)

    def turn(t, carry):
        at(t, multiply)
        for s in range(steps):
            at(t - 1 - SKEW * s, lambda c, s=s: forward(c, s))
        at(t - 1 - SKEW * steps, finish)
        return carry

    lax.fori_loop(0, chunks + 1 + SKEW * steps, turn, 0)

    def settle(c, carry):
        pair_copy(c).wait_send()
        for s in range(steps):
            @pl.when(z <= s)
            def _(s=s):
                up_copy(c, s).wait_send()

            @pl.when(z >= steps - s)
            def _(s=s):
                down_copy(c, s).wait_send()
        return carry

    lax.fori_loop(0, chunks, settle, 0)


def summed_gradient(grads, w, n, rows, cid):
    chips = n // 2
    model_width, width = w.shape
    cw = model_width // GRAD_CHUNKS
    steps = max(chips - 1, 1)
    all_rows = pltpu.VMEM((GRAD_CHUNKS, chips, rows, cw), BF16)
    hops = pltpu.VMEM((GRAD_CHUNKS, steps, rows, cw), BF16)
    pair_sem = pltpu.SemaphoreType.DMA((GRAD_CHUNKS,))
    hop_sem = pltpu.SemaphoreType.DMA((GRAD_CHUNKS, steps))
    vmem = pl.BlockSpec(memory_space=pltpu.VMEM)
    return pl.pallas_call(
        functools.partial(gradient_kernel, n, GRAD_CHUNKS),
        out_shape=jax.ShapeDtypeStruct((rows, model_width), F32),
        in_specs=[vmem, pl.BlockSpec(memory_space=pl.ANY)],
        out_specs=vmem,
        scratch_shapes=[pltpu.VMEM((2, cw, width), BF16)]
        + [all_rows] * 3
        + [hops] * 4
        + [pltpu.SemaphoreType.DMA((2,))]
        + [pair_sem] * 2
        + [hop_sem] * 4,
        compiler_params=pltpu.CompilerParams(
            collective_id=cid, has_side_effects=True, vmem_limit_bytes=48 * 1024 * 1024
        ),
        cost_estimate=pl.CostEstimate(
            flops=2 * rows * n * model_width * width,
            bytes_accessed=model_width * width * 12,
            transcendentals=0,
        ),
    )(grads, w)


def local(tokens, w_query, cotangent, task_embed, w_hidden, head_a, head_b, block_task):
    n_groups = lax.axis_size("dp")
    n_shards = lax.axis_size("tensor")
    chips = n_shards // 2
    shard = lax.axis_index("tensor")
    z, core = shard // 2, shard % 2
    hid_count, rank_rows, width = head_a.shape
    rank = rank_rows * n_groups
    blocks = block_task.shape[0]
    per_group = blocks // n_groups
    rows_dev, model_width = tokens.shape
    rows_all = rows_dev * n_shards
    block = rows_all // per_group

    whole = lax.all_gather(tokens, "tensor", axis=0, tiled=True)

    by_core = cotangent.reshape(chips, 2, rows_dev, width)
    by_core = jnp.where(core == 0, by_core[:, ::-1], by_core)
    by_core = jnp.swapaxes(by_core, 0, 1).reshape(2, chips * rows_dev, width)
    frozen = summed_gradient(by_core, w_query, n_shards, rows_dev, 6)

    part = jax.nn.silu(
        jnp.dot(task_embed[block_task], w_hidden, preferred_element_type=F32)
    ).astype(BF16)
    hidden = exchange(part.astype(F32), "tensor", n_shards, False, 0)
    hidden = jnp.swapaxes(hidden, 0, 1).reshape(blocks, hid_count).astype(BF16)

    def generate(head):
        made = jnp.dot(
            hidden, head.reshape(hid_count, rank_rows * width), preferred_element_type=F32
        )
        return made.astype(BF16).astype(F32).reshape(n_groups, per_group, rank_rows, width)

    made = jnp.stack([generate(head_a), generate(head_b)], 1)
    made = made.reshape(n_groups, 2 * per_group * rank_rows, width)
    made = exchange(made, "dp", n_groups, True, 1).astype(BF16)
    made = made.reshape(n_groups, 2, per_group, rank_rows, width)
    made = made.transpose(1, 2, 0, 3, 4).reshape(2, per_group, rank, width)
    down_weight, up_weight = made[0], made[1]
    full_a = exchange(down_weight.reshape(per_group * rank, width), "tensor", n_shards, False, 2).astype(BF16)
    full_a = jnp.swapaxes(full_a, 0, 1).reshape(per_group, rank, model_width)
    which = shard * rows_dev // block
    a_here = lax.dynamic_index_in_dim(full_a, which, 0, keepdims=False)

    grads_in = cotangent.reshape(per_group, block, width)
    back_part = jnp.einsum("gps,grs->pgr", up_weight, grads_in, preferred_element_type=F32)
    down_own = jnp.einsum("ps,rs->pr", a_here, tokens, preferred_element_type=F32)
    both_parts = jnp.concatenate([back_part.reshape(rank, rows_all), down_own], 1)
    both_parts = exchange(both_parts, "tensor", n_shards, False, 3)
    back_low = both_parts[:, :, :rows_all].sum(0).astype(BF16)
    down_low = jnp.swapaxes(both_parts[:, :, rows_all:], 0, 1).reshape(rank, rows_all).astype(BF16)

    base = jnp.dot(whole, w_query, preferred_element_type=F32)
    update = jnp.einsum(
        "pgr,gpn->grn",
        down_low.reshape(rank, per_group, block),
        up_weight,
        preferred_element_type=F32,
    ).reshape(rows_all, width)
    output = (base + update).astype(BF16)

    back_here = lax.dynamic_slice_in_dim(back_low, shard * rows_dev, rows_dev, 1)
    grad_tokens = (
        frozen
        + jnp.einsum("pr,pd->rd", back_here, a_here, preferred_element_type=F32)
    ).astype(BF16)

    scale = 1.0 / block
    columns = lax.dynamic_slice_in_dim(whole, shard * width, width, 1)
    grad_a = jnp.einsum(
        "pgr,grd->pgd",
        back_low.reshape(rank, per_group, block),
        columns.reshape(per_group, block, width),
        preferred_element_type=F32,
    )
    grad_b = jnp.einsum(
        "pgr,grd->pgd",
        down_low.reshape(rank, per_group, block),
        grads_in,
        preferred_element_type=F32,
    )

    def send_back(grad, cid):
        low = (grad * scale).astype(BF16).astype(F32)
        low = low.reshape(n_groups, rank_rows * per_group, width)
        got = exchange(low, "dp", n_groups, True, cid)
        got = got.reshape(n_groups, rank_rows, per_group, width)
        return jnp.swapaxes(got, 1, 2).reshape(blocks, rank_rows, width)

    hid_f = hidden.astype(F32)

    def head_grad(got):
        return sum(
            hid_f[b][:, None, None] * got[b][None] for b in range(blocks)
        ).astype(BF16)

    grad_head_b = head_grad(send_back(grad_b, 4))
    grad_head_a = head_grad(send_back(grad_a, 5))
    return (output, grad_tokens, grad_head_a, grad_head_b)


def solution(mesh):
    return jax.shard_map(
        local,
        mesh=mesh,
        in_specs=(
            P(("dp", "tensor"), None),
            P(None, "tensor"),
            P("dp", "tensor"),
            P(),
            P(None, "tensor"),
            P(None, "dp", "tensor"),
            P(None, "dp", "tensor"),
            P(),
        ),
        out_specs=(
            P("dp", "tensor"),
            P(("dp", "tensor"), None),
            P(None, "dp", "tensor"),
            P(None, "dp", "tensor"),
        ),
        check_vma=False,
    )
```

time: 278 us -> 226 us (0.81)
  Pallas kernels: 0 us -> 153 us
  waiting for transfers between devices: 112 us -> 0.68 us
  blocking collectives: 61.1 us -> 0 us
  matrix products: 45.2 us -> 21.6 us
  other arithmetic: 1.66 us -> 20.9 us
  starting transfers between devices: 16.3 us -> 0.04 us
  local copies, waits for them, and re-layouts: 27.4 us -> 14.5 us
    pallas_call x0 -> x7, Pallas kernels: none -> 153 us  [the longest x1 77 us: summed_gradient(): pl.pallas_call(functools.partial(gradient_kernel, n, GRAD_CHUNKS), out_sh...]
    reduce_scatter x1 -> x0, waiting for transfers between devices: 97.1 us -> none  [local(): lax.psum_scatter(lax.dot_general(cotangent, w_query, (((1,), (1,)), ((),...]
    all_gather x2 -> x0, blocking collectives: 33.2 us -> none  [the longest x1 17.4 us: local(): full_a = lax.all_gather(adapter_down_weight, 'tensor', axis=2, tiled=True)]
    psum x1 -> x0, blocking collectives: 28 us -> none  [local(): down_projection = lax.psum(down_portion, 'tensor')]
    dot_general x13 -> x10, matrix products: 45.2 us -> 21.6 us  [the longest x1 13.4 us: local(): base = jnp.dot(whole, w_query, preferred_element_type=F32)]
    all_to_all x4 -> x0, starting transfers between devices: 16.2 us -> none  [the longest x1 4.2 us: local(): lax.all_to_all(gen_b, 'dp', split_axis=0, concat_axis=2, tiled=True)]
    convert_element_type x0 -> x3, other arithmetic: none -> 15.2 us  [the longest x1 13.5 us: head_grad(): return sum((hid_f[b][:, None, None] * got[b][None] for b in range(blocks)...]
    unnamed x17 -> x14, local copies, waits for them, and re-layouts: 24.8 us -> 9.91 us
  transfers between devices with their start and end apart: 6 -> 1, of which waited for: 3 -> 0; matrix products, arithmetic and copies ran while one was open for 25% -> 12% of each run, Pallas kernels for 0% -> 65%
where the time goes in v1:
time: 226 us; the launch traced here: 225 us
  Pallas kernels  153 us (68%)
  matrix products  21.6 us (10%)
  other arithmetic  20.9 us (9%)
  local copies, waits for them, and re-layouts  14.5 us (6%)
  between operations  14.3 us (6%)
    pallas_call x1, Pallas kernels, summed_gradient(): pl.pallas_call(functools.partial(gradient_kernel, n, GRAD_CHUNKS), out_sh...  77 us
    pallas_call x6, Pallas kernels, exchange(): pl.pallas_call(functools.partial(exchange_kernel, axis, n, scatter), out_...  76 us
    convert_element_type x1, other arithmetic, head_grad(): return sum((hid_f[b][:, None, None] * got[b][None] for b in range(blocks)...  13.5 us
    dot_general x1, matrix products, local(): base = jnp.dot(whole, w_query, preferred_element_type=F32)  13.4 us
    unnamed x14, local copies, waits for them, and re-layouts  9.91 us
  transfers between devices with their start and end apart: 1, of which 0 were waited for; matrix products, arithmetic and copies ran while one was open for 12% of the time, Pallas kernels for 65%

profile of v1, /device:TPU:0, one launch (start us, length us, event | category | flops | bytes accessed | tf_op | source)
XLA Modules:
  0.0 225.0 jit_solution(6566163293876339419)
XLA Ops:
  7.2 0.7 all-gather.2.cloned.1.call-update
  9.2 1.0 fusion.9
  10.8 8.7 %shard_map.111 = f32[8,8,128]{2,1,0:T(8,128)} custom-call(f32[8,128]{1,0:T(8,128)} %pad_convert_fusion.2.x_ref), custom_call_target="tpu_custom_call" | custom-call | tf_op jit(solution)/shard_map/pallas_call | solution.py:48
  19.5 0.8 fusion.12
  20.4 5.2 %copy.27 = bf16[64,8,4,1024]{3,1,2,0:T(8,128)(2,1)S(1)} copy(bf16[64,8,4,1024]{3,2,1,0:T(4,128)(2,1)} %bitcast.76) | data formatting | bytes 8388608
  26.3 4.7 %copy.26 = bf16[64,8,4,1024]{3,1,2,0:T(8,128)(2,1)S(1)} copy(bf16[64,8,4,1024]{3,2,1,0:T(4,128)(2,1)} %bitcast.77) | data formatting | bytes 8388608
  31.7 0.7 reshape.117.x_ref
  32.4 6.8 %shard_map.112 = f32[4,8,1024]{2,1,0:T(8,128)} custom-call(f32[4,8,1024]{2,1,0:T(8,128)} %reshape.117.x_ref), custom_call_target="tpu_custom_call" | custom-call | tf_op jit(solution)/shard_map/pallas_call | solution.py:48
  39.3 0.9 convert_element_type.108
  40.9 22.9 %shard_map.113 = f32[8,16,1024]{2,1,0:T(8,128)} custom-call(f32[16,1024]{1,0:T(8,128)} %reshape.118.x_ref), custom_call_target="tpu_custom_call" | custom-call | tf_op jit(solution)/shard_map/pallas_call | solution.py:48
  63.8 1.1 convert_bitcast_fusion
  66.3 23.7 %shard_map.114 = f32[8,16,640]{2,1,0:T(8,128)} custom-call(f32[16,640]{1,0:T(8,128)} %select_maximum_fusion.x_ref), custom_call_target="tpu_custom_call" | custom-call | tf_op jit(solution)/shard_map/pallas_call | solution.py:48
  90.0 0.8 fusion.6
  92.0 7.2 %shard_map.117 = f32[4,8,1024]{2,1,0:T(8,128)} custom-call(f32[4,8,1024]{2,1,0:T(8,128)} %pad_convert_fusion.x_ref), custom_call_target="tpu_custom_call" | custom-call | tf_op jit(solution)/shard_map/pallas_call | solution.py:48
  99.6 1.0 slice_reduce_fusion
  100.8 1.9 fusion.17
  102.7 77.0 %shard_map.115 = f32[64,8192]{1,0:T(8,128)S(1)} custom-call(bf16[2,256,1024]{2,1,0:T(8,128)(2,1)S(1)} %bitcast.72, bf16[8192,1024]{1,0:T(8,128)(2,1)} %w_ref.1), custom_call_target="tpu_custom_call" | custom-call | flops 8589934592 | bytes 100663296 | tf_op jit(solution)/shard_map/pallas_call | solution.py:235
  179.7 1.5 fusion
  181.2 1.5 fusion.3
  182.7 0.7 pad_convert_fusion.1.x_ref
  183.4 6.8 %shard_map.116 = f32[4,8,1024]{2,1,0:T(8,128)} custom-call(f32[4,8,1024]{2,1,0:T(8,128)} %pad_convert_fusion.1.x_ref), custom_call_target="tpu_custom_call" | custom-call | tf_op jit(solution)/shard_map/pallas_call | solution.py:48
  190.2 1.0 slice_bitcast_fusion.3
  191.1 13.5 %add_convert_fusion = (bf16[512,4,1024]{2,1,0:T(4,128)(2,1)}, bf16[512,4,1024]{2,1,0:T(4,128)(2,1)}) fusion(f32[4,1024]{1,0:T(4,128)S(1)} %get-tuple-element.11, f32[4,1024]{1,0:T(4,128)S(1)} %get-tuple-element.12, f32[4,1024]{1,0:T(4,128)S(1)} %get-tuple-element.13, f32[4,1024]{1,0:T(4,128)S(1)} %get-tuple-element.10, f32[512]{0:T(512)S(1)} %mul.161, ...), kind=kLoop, calls=%fused_computation.3 | loop fusion | flops 33554432 | bytes 8527872 | tf_op jit(solution)/shard_map/convert_element_type | solution.py:351
  204.7 13.4 %add_convert_fusion.2 = bf16[512,1024]{1,0:T(8,128)(2,1)} fusion(f32[512,1024]{1,0:T(8,128)S(1)} %copy-done.3, bf16[512,8192]{1,0:T(8,128)(2,1)S(1)} %copy-done.5, bf16[8192,1024]{1,0:T(8,128)(2,1)} %w_ref.1), kind=kOutput, calls=%fused_computation.7 | convolution fusion | flops 8590983168 | bytes 28311552 | tf_op jit(solution)/shard_map/dot_general | solution.py:309
  (47 shorter events, 7.4 us)
Async XLA Ops:
  7.2 1.4 copy-start
  7.2 174.0 %all-gather.2.cloned.1.call-start = ((), (), s32[]{:S(2)}) async-start(), calls=%async_computation | async-start | bytes 9437184 | tf_op jit(solution)/shard_map/all_gather | solution.py:271
  26.3 38.7 %copy-start.1 = (bf16[512,1024]{1,0:T(8,128)(2,1)S(1)}, bf16[512,1024]{1,0:T(8,128)(2,1)}, u32[]{:S(2)}) copy-start(bf16[512,1024]{1,0:T(8,128)(2,1)} %param.10) | copy-start | bytes 3145732
  26.3 39.0 %copy-start.2 = (bf16[64,8192]{1,0:T(8,128)(2,1)S(1)}, bf16[64,8192]{1,0:T(8,128)(2,1)}, u32[]{:S(2)}) copy-start(bf16[64,8192]{1,0:T(8,128)(2,1)} %param.8) | copy-start | bytes 3145732
  102.7 87.5 %copy-start.4 = (f32[4,8,1024]{2,1,0:T(8,128)S(1)}, f32[4,8,1024]{2,1,0:T(8,128)}, u32[]{:S(2)}) copy-start(f32[4,8,1024]{2,1,0:T(8,128)} %shard_map.117) | copy-start | bytes 393220
  179.7 25.0 %copy-start.3 = (f32[512,1024]{1,0:T(8,128)S(1)}, f32[512,1024]{1,0:T(8,128)}, u32[]{:S(2)}) copy-start(f32[512,1024]{1,0:T(8,128)} %fusion.17) | copy-start | bytes 6291460
  190.2 14.5 %copy-start.5 = (bf16[512,8192]{1,0:T(8,128)(2,1)S(1)}, bf16[512,8192]{1,0:T(8,128)(2,1)}, u32[]{:S(2)}) copy-start(bf16[512,8192]{1,0:T(8,128)(2,1)} %all-gather.2.cloned.1.call-done) | copy-start | bytes 25165828
Sparse Core Ops, SparseCore 0:
  9.6 102.7 all-gather.1

commit v2 on v1

--- a/solution.py
+++ b/solution.py
@@ -274,6 +274,7 @@
     by_core = jnp.where(core == 0, by_core[:, ::-1], by_core)
     by_core = jnp.swapaxes(by_core, 0, 1).reshape(2, chips * rows_dev, width)
     frozen = summed_gradient(by_core, w_query, n_shards, rows_dev, 6)
+    frozen, task_embed = lax.optimization_barrier((frozen, task_embed))
 
     part = jax.nn.silu(
         jnp.dot(task_embed[block_task], w_hidden, preferred_element_type=F32)
@@ -336,12 +337,13 @@
         preferred_element_type=F32,
     )
 
-    def send_back(grad, cid):
-        low = (grad * scale).astype(BF16).astype(F32)
-        low = low.reshape(n_groups, rank_rows * per_group, width)
-        got = exchange(low, "dp", n_groups, True, cid)
-        got = got.reshape(n_groups, rank_rows, per_group, width)
-        return jnp.swapaxes(got, 1, 2).reshape(blocks, rank_rows, width)
+    low = (jnp.stack([grad_a, grad_b]) * scale).astype(BF16).astype(F32)
+    low = jnp.swapaxes(low.reshape(2, n_groups, rank_rows * per_group, width), 0, 1)
+    got = exchange(
+        low.reshape(n_groups, 2 * rank_rows * per_group, width), "dp", n_groups, True, 4
+    )
+    got = got.reshape(n_groups, 2, rank_rows, per_group, width)
+    got = got.transpose(1, 0, 3, 2, 4).reshape(2, blocks, rank_rows, width)
 
     hid_f = hidden.astype(F32)
 
@@ -350,8 +352,8 @@
             hid_f[b][:, None, None] * got[b][None] for b in range(blocks)
         ).astype(BF16)
 
-    grad_head_b = head_grad(send_back(grad_b, 4))
-    grad_head_a = head_grad(send_back(grad_a, 5))
+    grad_head_b = head_grad(got[1])
+    grad_head_a = head_grad(got[0])
     return (output, grad_tokens, grad_head_a, grad_head_b)
 
 

time: 226 us -> 264 us (1.17)
  Pallas kernels: 153 us -> 188 us
  local copies, waits for them, and re-layouts: 14.5 us -> 17.4 us
    pallas_call x1, Pallas kernels: 77 us -> 137 us  [summed_gradient(): pl.pallas_call(functools.partial(gradient_kernel, n, GRAD_CHUNKS), out_sh...]
    pallas_call x6 -> x5, Pallas kernels: 76 us -> 50.1 us  [exchange(): pl.pallas_call(functools.partial(exchange_kernel, axis, n, scatter), out_...]
  transfers between devices with their start and end apart: 1 -> 1, of which waited for: 0 -> 0; matrix products, arithmetic and copies ran while one was open for 12% -> 11% of each run, Pallas kernels for 65% -> 69%
where the time goes in v2:
time: 264 us; the launch traced here: 263 us
  Pallas kernels  188 us (71%)
  matrix products  23.1 us (9%)
  other arithmetic  19.9 us (8%)
  local copies, waits for them, and re-layouts  17.4 us (7%)
  between operations  14.3 us (5%)
    pallas_call x1, Pallas kernels, summed_gradient(): pl.pallas_call(functools.partial(gradient_kernel, n, GRAD_CHUNKS), out_sh...  137 us
    pallas_call x5, Pallas kernels, exchange(): pl.pallas_call(functools.partial(exchange_kernel, axis, n, scatter), out_...  50.1 us
    convert_element_type x1, other arithmetic, head_grad(): return sum((hid_f[b][:, None, None] * got[b][None] for b in range(blocks)...  13.7 us
    dot_general x1, matrix products, local(): base = jnp.dot(whole, w_query, preferred_element_type=F32)  13.4 us
    unnamed x14, local copies, waits for them, and re-layouts  8.99 us
  transfers between devices with their start and end apart: 1, of which 0 were waited for; matrix products, arithmetic and copies ran while one was open for 11% of the time, Pallas kernels for 69%

profile of v2, /device:TPU:0, one launch (start us, length us, event | category | flops | bytes accessed | tf_op | source)
XLA Modules:
  0.0 262.9 jit_solution(10693245610802302320)
XLA Ops:
  7.9 1.3 copy.19
  9.5 137.5 %shard_map.111 = f32[64,8192]{1,0:T(8,128)S(1)} custom-call(bf16[2,256,1024]{2,1,0:T(8,128)(2,1)S(1)} %bitcast.77, bf16[8192,1024]{1,0:T(8,128)(2,1)} %w_ref.1), custom_call_target="tpu_custom_call" | custom-call | flops 8589934592 | bytes 100663296 | tf_op jit(solution)/shard_map/pallas_call | solution.py:235
  148.4 9.2 %shard_map.112 = f32[8,8,128]{2,1,0:T(8,128)} custom-call(f32[8,128]{1,0:T(8,128)} %pad_convert_fusion.x_ref), custom_call_target="tpu_custom_call" | custom-call | tf_op jit(solution)/shard_map/pallas_call | solution.py:48
  157.6 0.8 fusion.9
  158.5 4.5 %copy.31 = bf16[64,8,4,1024]{3,1,2,0:T(8,128)(2,1)S(1)} copy(bf16[64,8,4,1024]{3,2,1,0:T(4,128)(2,1)} %bitcast.81) | data formatting | bytes 8388608
  164.3 4.5 %copy.30 = bf16[64,8,4,1024]{3,1,2,0:T(8,128)(2,1)S(1)} copy(bf16[64,8,4,1024]{3,2,1,0:T(4,128)(2,1)} %bitcast.82) | data formatting | bytes 8388608
  170.1 0.8 maximum_convert_fusion
  170.9 0.7 reshape.145.x_ref
  171.6 6.9 %shard_map.113 = f32[4,8,1024]{2,1,0:T(8,128)} custom-call(f32[4,8,1024]{2,1,0:T(8,128)} %reshape.145.x_ref), custom_call_target="tpu_custom_call" | custom-call | tf_op jit(solution)/shard_map/pallas_call | solution.py:48
  178.5 0.9 convert_element_type.88
  180.2 13.5 %shard_map.114 = f32[8,16,1024]{2,1,0:T(8,128)} custom-call(f32[16,1024]{1,0:T(8,128)} %reshape.146.x_ref), custom_call_target="tpu_custom_call" | custom-call | tf_op jit(solution)/shard_map/pallas_call | solution.py:48
  193.7 1.1 convert_bitcast_fusion
  194.7 0.7 copy.29
  195.9 1.7 fusion.13
  198.2 13.2 %shard_map.115 = f32[8,16,640]{2,1,0:T(8,128)} custom-call(f32[16,640]{1,0:T(8,128)} %select_maximum_fusion.x_ref), custom_call_target="tpu_custom_call" | custom-call | tf_op jit(solution)/shard_map/pallas_call | solution.py:48
  211.5 0.8 fusion.3
  213.1 1.0 slice_reduce_fusion
  214.0 1.8 fusion.14
  215.9 2.4 fusion
  218.3 1.6 convolution_bitcast_fusion
  220.7 7.2 %shard_map.116 = f32[4,8,1024]{2,1,0:T(8,128)} custom-call(f32[4,8,1024]{2,1,0:T(8,128)} %reshape.148.x_ref), custom_call_target="tpu_custom_call" | custom-call | tf_op jit(solution)/shard_map/pallas_call | solution.py:48
  228.0 0.9 reshape.143
  228.9 13.7 %add_convert_fusion = (bf16[512,4,1024]{2,1,0:T(4,128)(2,1)}, bf16[512,4,1024]{2,1,0:T(4,128)(2,1)}) fusion(f32[4,1024]{1,0:T(4,128)S(1)} %get-tuple-element.15, f32[4,1024]{1,0:T(4,128)S(1)} %get-tuple-element.16, f32[4,1024]{1,0:T(4,128)S(1)} %get-tuple-element.17, f32[4,1024]{1,0:T(4,128)S(1)} %get-tuple-element.14, f32[512]{0:T(512)S(1)} %mul.160, ...), kind=kLoop, calls=%fused_computation.3 | loop fusion | flops 33554432 | bytes 8527872 | tf_op jit(solution)/shard_map/convert_element_type | solution.py:353
  242.7 13.4 %add_convert_fusion.2 = bf16[512,1024]{1,0:T(8,128)(2,1)} fusion(f32[512,1024]{1,0:T(8,128)S(1)} %copy-done.2, bf16[512,8192]{1,0:T(8,128)(2,1)S(1)} %copy-done.3, bf16[8192,1024]{1,0:T(8,128)(2,1)} %w_ref.1), kind=kOutput, calls=%fused_computation.7 | convolution fusion | flops 8590983168 | bytes 28311552 | tf_op jit(solution)/shard_map/dot_general | solution.py:310
  (47 shorter events, 8.4 us)
Async XLA Ops:
  7.2 139.9 %copy-start = (bf16[128,1024]{1,0:T(8,128)(2,1)S(1)}, bf16[128,1024]{1,0:T(8,128)(2,1)}, u32[]{:S(2)}) copy-start(bf16[128,1024]{1,0:T(8,128)(2,1)} %param.11) | copy-start | bytes 786436
  7.2 211.1 %all-gather.2.cloned.1.call-start = ((), (), s32[]{:S(2)}) async-start(), calls=%async_computation | async-start | bytes 9437184 | tf_op jit(solution)/shard_map/all_gather | solution.py:271
  9.5 137.5 %copy-start.5 = (s32[4]{0:T(128)S(1)}, s32[4]{0:T(128)}, u32[]{:S(2)}) copy-start(s32[4]{0:T(128)} %param.15) | copy-start | bytes 52
  9.5 138.1 %copy-start.4 = (bf16[1024,64]{0,1:T(8,128)(2,1)S(1)}, bf16[1024,64]{0,1:T(8,128)(2,1)}, u32[]{:S(2)}) copy-start(bf16[1024,64]{0,1:T(8,128)(2,1)} %param.12) | copy-start | bytes 393220
  163.6 31.9 %copy-start.1 = (bf16[512,1024]{1,0:T(8,128)(2,1)S(1)}, bf16[512,1024]{1,0:T(8,128)(2,1)}, u32[]{:S(2)}) copy-start(bf16[512,1024]{1,0:T(8,128)(2,1)} %param.10) | copy-start | bytes 3145732
  218.3 24.3 %copy-start.2 = (f32[512,1024]{1,0:T(8,128)S(1)}, f32[512,1024]{1,0:T(8,128)}, u32[]{:S(2)}) copy-start(f32[512,1024]{1,0:T(8,128)} %fusion.14) | copy-start | bytes 6291460
  228.9 13.8 %copy-start.3 = (bf16[512,8192]{1,0:T(8,128)(2,1)S(1)}, bf16[512,8192]{1,0:T(8,128)(2,1)}, u32[]{:S(2)}) copy-start(bf16[512,8192]{1,0:T(8,128)(2,1)} %all-gather.2.cloned.1.call-done) | copy-start | bytes 25165828
Sparse Core Ops, SparseCore 0:
  9.6 140.9 all-gather.1

commit v3 on v2

--- a/solution.py
+++ b/solution.py
@@ -274,7 +274,6 @@
     by_core = jnp.where(core == 0, by_core[:, ::-1], by_core)
     by_core = jnp.swapaxes(by_core, 0, 1).reshape(2, chips * rows_dev, width)
     frozen = summed_gradient(by_core, w_query, n_shards, rows_dev, 6)
-    frozen, task_embed = lax.optimization_barrier((frozen, task_embed))
 
     part = jax.nn.silu(
         jnp.dot(task_embed[block_task], w_hidden, preferred_element_type=F32)

time: 264 us -> 218 us (0.83)
  Pallas kernels: 188 us -> 146 us
    pallas_call x1, Pallas kernels: 137 us -> 77.5 us  [summed_gradient(): pl.pallas_call(functools.partial(gradient_kernel, n, GRAD_CHUNKS), out_sh...]
    pallas_call x5, Pallas kernels: 50.1 us -> 68.9 us  [exchange(): pl.pallas_call(functools.partial(exchange_kernel, axis, n, scatter), out_...]
    unnamed x14 -> x12, local copies, waits for them, and re-layouts: 8.99 us -> 9.91 us
  transfers between devices with their start and end apart: 1 -> 1, of which waited for: 0 -> 0; matrix products, arithmetic and copies ran while one was open for 11% -> 12% of each run, Pallas kernels for 69% -> 64%
where the time goes in v3:
time: 218 us
  Pallas kernels  146 us (67%)
  matrix products  21.6 us (10%)
  other arithmetic  19.4 us (9%)
  local copies, waits for them, and re-layouts  15.2 us (7%)
  between operations  14.3 us (7%)
    pallas_call x1, Pallas kernels, summed_gradient(): pl.pallas_call(functools.partial(gradient_kernel, n, GRAD_CHUNKS), out_sh...  77.5 us
    pallas_call x5, Pallas kernels, exchange(): pl.pallas_call(functools.partial(exchange_kernel, axis, n, scatter), out_...  68.9 us
    dot_general x1, matrix products, local(): base = jnp.dot(whole, w_query, preferred_element_type=F32)  13.4 us
    convert_element_type x1, other arithmetic, head_grad(): return sum((hid_f[b][:, None, None] * got[b][None] for b in range(blocks)...  13.4 us
    unnamed x12, local copies, waits for them, and re-layouts  9.91 us
  transfers between devices with their start and end apart: 1, of which 0 were waited for; matrix products, arithmetic and copies ran while one was open for 12% of the time, Pallas kernels for 64%

profile of v3, /device:TPU:0, one launch (start us, length us, event | category | flops | bytes accessed | tf_op | source)
XLA Modules:
  0.0 217.6 jit_solution(9798649385933301162)
XLA Ops:
  7.2 0.7 all-gather.2.cloned.1.call-update
  7.9 0.7 compare_select_fusion
  9.2 1.0 fusion.6
  10.8 8.7 %shard_map.111 = f32[8,8,128]{2,1,0:T(8,128)} custom-call(f32[8,128]{1,0:T(8,128)} %pad_convert_fusion.x_ref), custom_call_target="tpu_custom_call" | custom-call | tf_op jit(solution)/shard_map/pallas_call | solution.py:48
  19.5 0.8 fusion.9
  20.4 5.2 %copy.31 = bf16[64,8,4,1024]{3,1,2,0:T(8,128)(2,1)S(1)} copy(bf16[64,8,4,1024]{3,2,1,0:T(4,128)(2,1)} %bitcast.81) | data formatting | bytes 8388608
  26.3 4.7 %copy.30 = bf16[64,8,4,1024]{3,1,2,0:T(8,128)(2,1)S(1)} copy(bf16[64,8,4,1024]{3,2,1,0:T(4,128)(2,1)} %bitcast.82) | data formatting | bytes 8388608
  31.7 0.7 reshape.145.x_ref
  32.4 6.8 %shard_map.112 = f32[4,8,1024]{2,1,0:T(8,128)} custom-call(f32[4,8,1024]{2,1,0:T(8,128)} %reshape.145.x_ref), custom_call_target="tpu_custom_call" | custom-call | tf_op jit(solution)/shard_map/pallas_call | solution.py:48
  39.3 0.9 convert_element_type.88
  40.9 22.9 %shard_map.113 = f32[8,16,1024]{2,1,0:T(8,128)} custom-call(f32[16,1024]{1,0:T(8,128)} %reshape.146.x_ref), custom_call_target="tpu_custom_call" | custom-call | tf_op jit(solution)/shard_map/pallas_call | solution.py:48
  63.8 1.1 convert_bitcast_fusion
  66.3 23.7 %shard_map.114 = f32[8,16,640]{2,1,0:T(8,128)} custom-call(f32[16,640]{1,0:T(8,128)} %select_maximum_fusion.x_ref), custom_call_target="tpu_custom_call" | custom-call | tf_op jit(solution)/shard_map/pallas_call | solution.py:48
  90.0 0.8 fusion.3
  91.7 1.0 slice_reduce_fusion
  92.9 1.9 fusion.14
  94.8 77.5 %shard_map.115 = f32[64,8192]{1,0:T(8,128)S(1)} custom-call(bf16[2,256,1024]{2,1,0:T(8,128)(2,1)S(1)} %bitcast.77, bf16[8192,1024]{1,0:T(8,128)(2,1)} %w_ref.1), custom_call_target="tpu_custom_call" | custom-call | flops 8589934592 | bytes 100663296 | tf_op jit(solution)/shard_map/pallas_call | solution.py:235
  172.4 1.5 fusion
  173.9 1.5 convolution_bitcast_fusion
  175.4 0.7 reshape.148.x_ref
  176.1 6.9 %shard_map.116 = f32[4,8,1024]{2,1,0:T(8,128)} custom-call(f32[4,8,1024]{2,1,0:T(8,128)} %reshape.148.x_ref), custom_call_target="tpu_custom_call" | custom-call | tf_op jit(solution)/shard_map/pallas_call | solution.py:48
  183.0 0.9 reshape.143
  184.0 13.4 %add_convert_fusion = (bf16[512,4,1024]{2,1,0:T(4,128)(2,1)}, bf16[512,4,1024]{2,1,0:T(4,128)(2,1)}) fusion(f32[4,1024]{1,0:T(4,128)S(1)} %get-tuple-element.11, f32[4,1024]{1,0:T(4,128)S(1)} %get-tuple-element.12, f32[4,1024]{1,0:T(4,128)S(1)} %get-tuple-element.13, f32[4,1024]{1,0:T(4,128)S(1)} %get-tuple-element.10, f32[512]{0:T(512)S(1)} %mul.160, ...), kind=kLoop, calls=%fused_computation.3 | loop fusion | flops 33554432 | bytes 8527872 | tf_op jit(solution)/shard_map/convert_element_type | solution.py:352
  197.3 13.4 %add_convert_fusion.2 = bf16[512,1024]{1,0:T(8,128)(2,1)} fusion(f32[512,1024]{1,0:T(8,128)S(1)} %copy-done.3, bf16[512,8192]{1,0:T(8,128)(2,1)S(1)} %copy-done.4, bf16[8192,1024]{1,0:T(8,128)(2,1)} %w_ref.1), kind=kOutput, calls=%fused_computation.7 | convolution fusion | flops 8590983168 | bytes 28311552 | tf_op jit(solution)/shard_map/dot_general | solution.py:309
  (45 shorter events, 6.1 us)
Async XLA Ops:
  7.2 1.4 copy-start
  7.2 166.7 %all-gather.2.cloned.1.call-start = ((), (), s32[]{:S(2)}) async-start(), calls=%async_computation | async-start | bytes 9437184 | tf_op jit(solution)/shard_map/all_gather | solution.py:271
  26.3 38.7 %copy-start.1 = (bf16[512,1024]{1,0:T(8,128)(2,1)S(1)}, bf16[512,1024]{1,0:T(8,128)(2,1)}, u32[]{:S(2)}) copy-start(bf16[512,1024]{1,0:T(8,128)(2,1)} %param.10) | copy-start | bytes 3145732
  26.3 39.0 %copy-start.2 = (bf16[64,8192]{1,0:T(8,128)(2,1)S(1)}, bf16[64,8192]{1,0:T(8,128)(2,1)}, u32[]{:S(2)}) copy-start(bf16[64,8192]{1,0:T(8,128)(2,1)} %param.8) | copy-start | bytes 3145732
  172.4 25.0 %copy-start.3 = (f32[512,1024]{1,0:T(8,128)S(1)}, f32[512,1024]{1,0:T(8,128)}, u32[]{:S(2)}) copy-start(f32[512,1024]{1,0:T(8,128)} %fusion.14) | copy-start | bytes 6291460
  183.9 13.4 %copy-start.4 = (bf16[512,8192]{1,0:T(8,128)(2,1)S(1)}, bf16[512,8192]{1,0:T(8,128)(2,1)}, u32[]{:S(2)}) copy-start(bf16[512,8192]{1,0:T(8,128)(2,1)} %all-gather.2.cloned.1.call-done) | copy-start | bytes 25165828
Sparse Core Ops, SparseCore 0:
  9.6 102.7 all-gather.1
